TPU v7x, 32 devices: a whole 2x2x4 slice. The times are simulated.
32 devices in a mesh: sess: 4 (over y, x), exp: 8 (over z, core).
Axes of the slice: x: 2, y: 2, z: 4, core: 2. Of those that a mesh axis runs over, the one named last changes fastest.
Arguments:
- tokens: bfloat16 [1024, 2048], P(('sess', 'exp')), may hold values from -6 to 6
- thinker_gain: float32 [2048], replicated, may hold values from 0.25 to 1.75
- thinker_ids: int32 [1024, 8], P(('sess', 'exp')), may hold values from 0 to 7, all different within a row; in each aligned block of 32 rows (0 to 31, 32 to 63, ...) at most 32 rows name the same one
- thinker_gates: float32 [1024, 8], P(('sess', 'exp')), may hold values from 0.05 to 0.25
- w_gate: bfloat16 [8, 2048, 768], P('exp'), may hold values from -0.125 to 0.125
- w_up: bfloat16 [8, 2048, 768], P('exp'), may hold values from -0.125 to 0.125
- w_down: bfloat16 [8, 768, 2048], P('exp'), may hold values from -0.21875 to 0.21875
- talker_in: bfloat16 [1024, 1024], P(('sess', 'exp')), may hold values from -6 to 6
- talker_gain: float32 [1024], replicated, may hold values from 0.25 to 1.75
- talker_ids: int32 [1024, 2], P(('sess', 'exp')), may hold values from 0 to 3, all different within a row; in each aligned block of 32 rows (0 to 31, 32 to 63, ...) at most 32 rows name the same one
- talker_gates: float32 [1024, 2], P(('sess', 'exp')), may hold values from 0.2 to 0.6
- t_gate: bfloat16 [4, 1024, 384], P('sess'), may hold values from -0.1875 to 0.1875
- t_up: bfloat16 [4, 1024, 384], P('sess'), may hold values from -0.1875 to 0.1875
- t_down: bfloat16 [4, 384, 1024], P('sess'), may hold values from -0.3125 to 0.3125
- conv_state: float32 [1024, 3, 1024], P(('sess', 'exp')), may hold values from -6 to 6
- conv_kernel: float32 [4, 1024], replicated, may hold values from -3 to 3
- conv_gain: float32 [1024], replicated, may hold values from 0.25 to 1.75
Outputs:
- thought: bfloat16 [1024, 2048], P(('sess', 'exp'))
- spoken: bfloat16 [1024, 1024], P(('sess', 'exp'))
- audio_frame: bfloat16 [1024, 1024], P(('sess', 'exp'))
- new_state: float32 [1024, 3, 1024], P(('sess', 'exp'))
Inputs may be any that keep to these rules, and one draw needn't show every extreme that they name: `thinker_ids`: each row names 8 different experts; within the 32 rows of one device no expert is named by more than 32 rows. `talker_ids`: each row names 2 different experts; within the 32 rows of one device no expert is named by more than 32 rows.
All inputs are finite; a program needn't handle non-finite values.
Results may differ from a plain program's by a relative error of at most 0.0055.
Values may be sent and summed in bfloat16 or wider, within the bound.
A program may use at most 64 MiB of HBM per device.

v0:
```python
import jax
import jax.numpy as jnp
from jax import lax
from jax.sharding import PartitionSpec as P


def rms_scale(values, gain):
    wide = values.astype(jnp.float32)
    scale = lax.rsqrt(jnp.mean(wide * wide, axis=-1, keepdims=True) + 1e-06)
    return (wide * scale * gain).astype(jnp.bfloat16)


def bucket_slots(ids, count):
    onehot = (ids[:, :, None] == jnp.arange(count, dtype=jnp.int32)).astype(jnp.int32)
    used = jnp.sum(onehot, axis=1, dtype=jnp.int32)
    before = jnp.cumsum(used, axis=0, dtype=jnp.int32) - used
    return jnp.sum(onehot * before[:, None, :], axis=2, dtype=jnp.int32)


def expert_rows(rows, weight_gate, weight_up, weight_down):
    gate = jnp.dot(rows, weight_gate, preferred_element_type=jnp.float32)
    up = jnp.dot(rows, weight_up, preferred_element_type=jnp.float32)
    hidden = (jax.nn.silu(gate) * up).astype(jnp.bfloat16)
    return jnp.dot(hidden, weight_down, preferred_element_type=jnp.float32).astype(jnp.bfloat16)


def fill_buckets(normed, places, count, capacity):
    grid = jnp.arange(count * capacity, dtype=jnp.int32)
    select = jnp.any(places[:, :, None] == grid, axis=1).astype(jnp.bfloat16)
    filled = jnp.einsum("tp,td->pd", select, normed, preferred_element_type=jnp.float32)
    return filled.astype(jnp.bfloat16).reshape(count, capacity, normed.shape[1])


def combine_back(values, returned, places, gates):
    flat = returned.reshape(-1, returned.shape[2])
    picked = jnp.take(flat, places.reshape(-1), axis=0).reshape(
        places.shape[0], places.shape[1], -1
    )
    total = jnp.sum(gates[:, :, None] * picked.astype(jnp.float32), axis=1)
    return (values.astype(jnp.float32) + total).astype(jnp.bfloat16)


def shards(
    tokens,
    thinker_gain,
    thinker_ids,
    thinker_gates,
    w_gate,
    w_up,
    w_down,
    talker_in,
    talker_gain,
    talker_ids,
    talker_gates,
    t_gate,
    t_up,
    t_down,
    conv_state,
    conv_kernel,
    conv_gain,
):
    sess_dev = tokens.shape[0]
    experts = lax.axis_size("exp") * w_gate.shape[0]
    owners = lax.axis_size("sess") * t_gate.shape[0]
    capacity = min(sess_dev, 2 * sess_dev * thinker_ids.shape[1] // experts)
    talk_capacity = min(sess_dev, 2 * sess_dev * talker_ids.shape[1] // owners)
    normed = rms_scale(tokens, thinker_gain)
    places = thinker_ids * capacity + bucket_slots(thinker_ids, experts)
    buckets = fill_buckets(normed, places, experts, capacity)
    rows = lax.all_to_all(buckets, "exp", split_axis=0, concat_axis=0, tiled=True)
    sources = rows.shape[0]
    slots_here = rows.shape[1]
    flat = rows.reshape(sources * slots_here, rows.shape[2])
    result = expert_rows(flat, w_gate[0], w_up[0], w_down[0]).reshape(sources, slots_here, -1)
    returned = lax.all_to_all(result, "exp", split_axis=0, concat_axis=0, tiled=True)
    thought = combine_back(tokens, returned, places, thinker_gates)
    normed = rms_scale(talker_in, talker_gain)
    places = talker_ids * talk_capacity + bucket_slots(talker_ids, owners)
    buckets = fill_buckets(normed, places, owners, talk_capacity)
    rows = lax.all_to_all(buckets, "sess", split_axis=0, concat_axis=0, tiled=True)
    sources = rows.shape[0]
    slots_here = rows.shape[1]
    flat = rows.reshape(sources * slots_here, rows.shape[2])
    result = expert_rows(flat, t_gate[0], t_up[0], t_down[0]).reshape(sources, slots_here, -1)
    returned = lax.all_to_all(result, "sess", split_axis=0, concat_axis=0, tiled=True)
    spoken = combine_back(talker_in, returned, places, talker_gates)
    window = jnp.concatenate([conv_state, spoken.astype(jnp.float32)[:, None, :]], axis=1)
    mixed = jnp.sum(window * conv_kernel[None, :, :], axis=1)
    scale = lax.rsqrt(jnp.mean(mixed * mixed, axis=-1, keepdims=True) + 1e-06)
    audio_frame = (mixed * scale * conv_gain).astype(jnp.bfloat16)
    new_state = window[:, 1:, :]
    return (thought, spoken, audio_frame, new_state)


def solution(mesh):
    placed = (
        P(("sess", "exp"), None),
        P(),
        P(("sess", "exp"), None),
        P(("sess", "exp"), None),
        P("exp", None, None),
        P("exp", None, None),
        P("exp", None, None),
        P(("sess", "exp"), None),
        P(),
        P(("sess", "exp"), None),
        P(("sess", "exp"), None),
        P("sess", None, None),
        P("sess", None, None),
        P("sess", None, None),
        P(("sess", "exp"), None, None),
        P(),
        P(),
    )
    return jax.shard_map(
        shards,
        mesh=mesh,
        in_specs=placed,
        out_specs=(
            P(("sess", "exp"), None),
            P(("sess", "exp"), None),
            P(("sess", "exp"), None),
            P(("sess", "exp"), None, None),
        ),
        check_vma=False,
    )
```

profile of v0, /device:TPU:0, one launch (start us, length us, event | category | flops | bytes accessed | tf_op | source)
XLA Modules:
  0.0 102.1 jit_solution(14677612758789205012)
XLA Ops:
  0.7 0.8 convert_reduce_fusion.1
  1.7 0.7 select_reduce_fusion.1
  3.2 1.0 fusion.37
  4.2 1.8 %convolution_convert_fusion.1 = bf16[128,1024]{1,0:T(8,128)(2,1)} fusion(pred[32,128]{1,0:T(8,128)(4,1)S(1)} %fusion.48, bf16[32,1024]{1,0:T(8,128)(2,1)} %param.24, f32[1024]{0:T(1024)} %param.25, f32[32]{0:T(128)S(1)} %add_rsqrt_fusion.1), kind=kOutput, calls=%fused_computation.13 | convolution fusion | flops 8650752 | bytes 336000 | tf_op jit(solution)/shard_map/tp,td->pd/dot_general | solution.py:30
  6.0 5.2 %all-to-all-start.2 = ((bf16[4,32,1024]{2,1,0:T(8,128)(2,1)}), bf16[4,32,1024]{2,1,0:T(8,128)(2,1)S(1)}, u32[]{:S(2)}, u32[]{:S(2)}) async-start(bf16[4,32,1024]{2,1,0:T(8,128)(2,1)} %bitcast.56), calls=%async_computation.2 | async-start | bytes 524288 | tf_op jit(solution)/shard_map/all_to_all | solution.py:80
  12.1 0.7 select_reduce_fusion
  13.7 1.0 %fusion.27 = f32[32]{0:T(128)S(1)} fusion(bf16[32,2048]{1,0:T(8,128)(2,1)} %param.17), kind=kLoop, calls=%fused_computation.32 | loop fusion | flops 196576 | bytes 131200 | tf_op jit(solution)/shard_map/reduce_sum | solution.py:9
  14.8 2.5 %convolution_convert_fusion = bf16[256,2048]{1,0:T(8,128)(2,1)} fusion(pred[32,256]{1,0:T(8,128)(4,1)S(1)} %fusion.31, bf16[32,2048]{1,0:T(8,128)(2,1)} %param.17, f32[2048]{0:T(1024)} %param.18, f32[32]{0:T(128)S(1)} %add_rsqrt_fusion.2), kind=kOutput, calls=%fused_computation.9 | convolution fusion | flops 34340864 | bytes 1196160 | tf_op jit(solution)/shard_map/tp,td->pd/dot_general | solution.py:30
  17.2 4.9 %all-to-all-start = ((bf16[8,32,2048]{2,1,0:T(8,128)(2,1)}), bf16[8,32,2048]{2,1,0:T(8,128)(2,1)}, u32[]{:S(2)}, u32[]{:S(2)}) async-start(bf16[8,32,2048]{2,1,0:T(8,128)(2,1)} %bitcast.52), calls=%async_computation | async-start | bytes 2097152 | tf_op jit(solution)/shard_map/all_to_all | solution.py:70
  22.8 2.1 %fusion.19 = f32[128,384]{1,0:T(8,128)} fusion(bf16[128,1024]{1,0:T(8,128)(2,1)S(1)} %bitcast.53, bf16[1,1024,384]{2,1,0:T(8,128)(2,1)} %param.28), kind=kOutput, calls=%fused_computation.20 | convolution fusion | flops 100663296 | bytes 1245184 | tf_op jit(solution)/shard_map/dot_general | solution.py:21
  24.9 2.8 %convolution_convert_fusion.2 = bf16[128,1024]{1,0:T(8,128)(2,1)} fusion(bf16[128,1024]{1,0:T(8,128)(2,1)S(1)} %bitcast.54, bf16[1,384,1024]{2,1,0:T(8,128)(2,1)} %param.30, bf16[1,1024,384]{2,1,0:T(8,128)(2,1)} %param.29, f32[128,384]{1,0:T(8,128)} %fusion.19), kind=kOutput, calls=%fused_computation.14 | convolution fusion | flops 201752576 | bytes 2293760 | tf_op jit(solution)/shard_map/dot_general | solution.py:24
  27.7 21.2 %all-to-all-done = bf16[8,32,2048]{2,1,0:T(8,128)(2,1)} async-done(((bf16[8,32,2048]{2,1,0:T(8,128)(2,1)}), bf16[8,32,2048]{2,1,0:T(8,128)(2,1)}, u32[]{:S(2)}, u32[]{:S(2)}) %all-to-all-start) | async-done | bytes 1048608 | tf_op jit(solution)/shard_map/all_to_all | solution.py:70
  48.8 4.2 %all-to-all-start.3 = ((bf16[4,32,1024]{2,1,0:T(8,128)(2,1)}), bf16[4,32,1024]{2,1,0:T(8,128)(2,1)S(1)}, u32[]{:S(2)}, u32[]{:S(2)}) async-start(bf16[4,32,1024]{2,1,0:T(8,128)(2,1)} %bitcast.57), calls=%async_computation.3 | async-start | bytes 524288 | tf_op jit(solution)/shard_map/all_to_all | solution.py:85
  53.0 4.1 %fusion.4 = f32[256,768]{1,0:T(8,128)} fusion(bf16[256,2048]{1,0:T(8,128)(2,1)} %bitcast.1, bf16[1,2048,768]{2,1,0:T(8,128)(2,1)} %param.21), kind=kOutput, calls=%fused_computation.6 | convolution fusion | flops 805306368 | bytes 4980736 | tf_op jit(solution)/shard_map/dot_general | solution.py:21
  57.1 5.6 %fusion.6 = bf16[256,2048]{1,0:T(8,128)(2,1)} fusion(bf16[1,768,2048]{2,1,0:T(8,128)(2,1)S(1)} %copy-done, bf16[256,2048]{1,0:T(8,128)(2,1)} %bitcast.1, bf16[1,2048,768]{2,1,0:T(8,128)(2,1)} %param.22, f32[256,768]{1,0:T(8,128)} %fusion.4), kind=kOutput, calls=%fused_computation.8 | convolution fusion | flops 1612316672 | bytes 9175040 | tf_op jit(solution)/shard_map/dot_general | solution.py:24
  62.7 4.4 %all-to-all-start.1 = ((bf16[8,32,2048]{2,1,0:T(8,128)(2,1)}), bf16[8,32,2048]{2,1,0:T(8,128)(2,1)}, u32[]{:S(2)}, u32[]{:S(2)}) async-start(bf16[8,32,2048]{2,1,0:T(8,128)(2,1)} %bitcast.55), calls=%async_computation.1 | async-start | bytes 2097152 | tf_op jit(solution)/shard_map/all_to_all | solution.py:75
  67.1 1.4 %gather_fusion.1 = bf16[64,1024]{1,0:T(8,128)(2,1)} fusion(bf16[128,1024]{1,0:T(8,128)(2,1)S(1)} %bitcast.51, s32[1024]{0:T(1024)S(1)} %pad_clamp_fusion), kind=kCustom, calls=%fused_computation.1 | custom fusion | bytes 262400 | tf_op jit(solution)/shard_map/jit(_take)/gather | solution.py:36
  68.5 1.0 gather.15
  70.6 1.1 %fusion.24 = f32[32,1024]{1,0:T(8,128)S(1)} fusion(f32[32,1,1024]{2,0,1:T(8,128)S(1)} %get-tuple-element.4, f32[32,3,1024]{2,0,1:T(8,128)} %param.31, f32[4,1024]{1,0:T(4,128)S(1)} %copy-done.3), kind=kLoop, calls=%fused_computation.26 | loop fusion | flops 360448 | bytes 671744 | tf_op jit(solution)/shard_map/reduce_sum | solution.py:88
  71.8 1.7 %fusion.25 = f32[32,3,1024]{2,0,1:T(8,128)} fusion(f32[32,3,1024]{2,0,1:T(8,128)} %param.31, f32[32,1,1024]{2,0,1:T(8,128)S(1)} %get-tuple-element.4), kind=kLoop, calls=%fused_computation.27 | loop fusion | flops 98304 | bytes 917504 | tf_op jit(solution)/shard_map/concatenate | solution.py:87
  73.5 0.7 multiply_convert_fusion
  74.2 19.4 %all-to-all-done.1 = bf16[8,32,2048]{2,1,0:T(8,128)(2,1)} async-done(((bf16[8,32,2048]{2,1,0:T(8,128)(2,1)}), bf16[8,32,2048]{2,1,0:T(8,128)(2,1)}, u32[]{:S(2)}, u32[]{:S(2)}) %all-to-all-start.1) | async-done | bytes 1048608 | tf_op jit(solution)/shard_map/all_to_all | solution.py:75
  93.7 4.8 %gather_fusion = bf16[256,2048]{1,0:T(8,128)(2,1)} fusion(bf16[256,2048]{1,0:T(8,128)(2,1)} %bitcast.6, s32[1024]{0:T(1024)S(1)} %pad_clamp_fusion.1), kind=kCustom, calls=%fused_computation | custom fusion | bytes 2098176 | tf_op jit(solution)/shard_map/jit(_take)/gather | solution.py:36
  98.5 2.9 %multiply_reduce_fusion = f32[32,2048]{1,0:T(8,128)S(1)} fusion(bf16[256,2048]{1,0:T(8,128)(2,1)} %gather_fusion, f32[32,8]{1,0:T(8,128)S(1)} %copy.40, pred[32,8]{1,0:T(8,128)(4,1)S(1)} %copy.44), kind=kLoop, calls=%fused_computation.10 | loop fusion | flops 2031616 | bytes 1312000 | tf_op jit(solution)/shard_map/reduce_sum | solution.py:39
  (48 shorter events, 5.5 us)
Async XLA Ops:
  0.6 56.5 %copy-start = (bf16[1,768,2048]{2,1,0:T(8,128)(2,1)S(1)}, bf16[1,768,2048]{2,1,0:T(8,128)(2,1)}, u32[]{:S(2)}) copy-start(bf16[1,768,2048]{2,1,0:T(8,128)(2,1)} %param.23) | copy-start | bytes 9437188
  0.6 21.7 %copy-start.4 = (f32[32,8]{0,1:T(8,128)S(1)}, f32[32,8]{0,1:T(8,128)}, u32[]{:S(2)}) copy-start(f32[32,8]{0,1:T(8,128)} %param.20) | copy-start | bytes 3076
  0.7 22.0 %copy-start.6 = (f32[32,2]{0,1:T(2,128)S(1)}, f32[32,2]{0,1:T(2,128)}, u32[]{:S(2)}) copy-start(f32[32,2]{0,1:T(2,128)} %param.27) | copy-start | bytes 772
  6.0 11.2 %all-to-all-start.2 = ((bf16[4,32,1024]{2,1,0:T(8,128)(2,1)}), bf16[4,32,1024]{2,1,0:T(8,128)(2,1)S(1)}, u32[]{:S(2)}, u32[]{:S(2)}) async-start(bf16[4,32,1024]{2,1,0:T(8,128)(2,1)} %bitcast.56), calls=%async_computation.2 | async-start | bytes 524288 | tf_op jit(solution)/shard_map/all_to_all | solution.py:80
  17.2 31.6 %all-to-all-start = ((bf16[8,32,2048]{2,1,0:T(8,128)(2,1)}), bf16[8,32,2048]{2,1,0:T(8,128)(2,1)}, u32[]{:S(2)}, u32[]{:S(2)}) async-start(bf16[8,32,2048]{2,1,0:T(8,128)(2,1)} %bitcast.52), calls=%async_computation | async-start | bytes 2097152 | tf_op jit(solution)/shard_map/all_to_all | solution.py:70
  48.8 13.9 %all-to-all-start.3 = ((bf16[4,32,1024]{2,1,0:T(8,128)(2,1)}), bf16[4,32,1024]{2,1,0:T(8,128)(2,1)S(1)}, u32[]{:S(2)}, u32[]{:S(2)}) async-start(bf16[4,32,1024]{2,1,0:T(8,128)(2,1)} %bitcast.57), calls=%async_computation.3 | async-start | bytes 524288 | tf_op jit(solution)/shard_map/all_to_all | solution.py:85
  62.7 7.3 %copy-start.2 = (bf16[32,1024]{1,0:T(8,128)(2,1)S(1)}, bf16[32,1024]{1,0:T(8,128)(2,1)}, u32[]{:S(2)}) copy-start(bf16[32,1024]{1,0:T(8,128)(2,1)} %param.24) | copy-start | bytes 196612
  62.7 7.9 %copy-start.3 = (f32[4,1024]{1,0:T(4,128)S(1)}, f32[4,1024]{1,0:T(4,128)}, u32[]{:S(2)}) copy-start(f32[4,1024]{1,0:T(4,128)} %param.32) | copy-start | bytes 49156
  62.7 10.8 %copy-start.5 = (f32[1024]{0:T(1024)S(1)}, f32[1024]{0:T(1024)}, u32[]{:S(2)}) copy-start(f32[1024]{0:T(1024)} %param.33) | copy-start | bytes 12292
  62.7 31.0 %all-to-all-start.1 = ((bf16[8,32,2048]{2,1,0:T(8,128)(2,1)}), bf16[8,32,2048]{2,1,0:T(8,128)(2,1)}, u32[]{:S(2)}, u32[]{:S(2)}) async-start(bf16[8,32,2048]{2,1,0:T(8,128)(2,1)} %bitcast.55), calls=%async_computation.1 | async-start | bytes 2097152 | tf_op jit(solution)/shard_map/all_to_all | solution.py:75
  93.7 7.7 %copy-start.1 = (bf16[32,2048]{1,0:T(8,128)(2,1)S(1)}, bf16[32,2048]{1,0:T(8,128)(2,1)}, u32[]{:S(2)}) copy-start(bf16[32,2048]{1,0:T(8,128)(2,1)} %param.17) | copy-start | bytes 393220
where the time goes:
time: 103 us; the launch traced here: 102 us
  waiting for transfers between devices  40.6 us (39%)
  matrix products  18.8 us (18%)
  starting transfers between devices  18.6 us (18%)
  other arithmetic  15.1 us (15%)
  local copies, waits for them, and re-layouts  8.17 us (8%)
    all_to_all x1, waiting for transfers between devices, shards(): lax.all_to_all(buckets, 'exp', split_axis=0, concat_axis=0, tiled=True)  21.2 us
    all_to_all x1, waiting for transfers between devices, shards(): lax.all_to_all(result, 'exp', split_axis=0, concat_axis=0, tiled=True)  19.4 us
    dot_general x2, matrix products, expert_rows(): jnp.dot(hidden, weight_down, preferred_element_type=jnp.float32)  8.31 us
    gather x3, local copies, waits for them, and re-layouts, combine_back(): jnp.take(flat, places.reshape(-1), axis=0)  7.11 us
    dot_general x2, matrix products, expert_rows(): gate = jnp.dot(rows, weight_gate, preferred_element_type=jnp.float32)  6.23 us
    all_to_all x1, starting transfers between devices, shards(): lax.all_to_all(buckets, 'sess', split_axis=0, concat_axis=0, tiled=True)  5.16 us
    all_to_all x1, starting transfers between devices, shards(): lax.all_to_all(buckets, 'exp', split_axis=0, concat_axis=0, tiled=True)  4.88 us
    all_to_all x1, starting transfers between devices, shards(): lax.all_to_all(result, 'exp', split_axis=0, concat_axis=0, tiled=True)  4.37 us
  transfers between devices with their start and end apart: 4, of which 2 were waited for; matrix products, arithmetic and copies ran while one was open for 28% of the time, Pallas kernels for 0%

commit v1 on v0

v1 whole, which is shorter than its diff:
```python
import functools

import jax
import jax.numpy as jnp
from jax import lax
from jax.experimental import pallas as pl
from jax.experimental.pallas import tpu as pltpu
from jax.sharding import PartitionSpec as P

MESH = pl.DeviceIdType.MESH
CORES = 2


def rms_scale(values, gain):
    wide = values.astype(jnp.float32)
    scale = lax.rsqrt(jnp.mean(wide * wide, axis=-1, keepdims=True) + 1e-06)
    return (wide * scale * gain).astype(jnp.bfloat16)


def gate_table(ids, gates, count, width):
    sessions = ids.shape[1]
    row = lax.broadcasted_iota(jnp.int32, (width, sessions), 0)
    expert = jnp.where(row < count, row, row - count)
    table = jnp.zeros((width, sessions), jnp.float32)
    for k in range(ids.shape[0]):
        table = table + jnp.where(expert == ids[k : k + 1, :], gates[k : k + 1, :], 0.0)
    table = jnp.where(row < 2 * count, table, 0.0)
    high = table.astype(jnp.bfloat16)
    low = (table - high.astype(jnp.float32)).astype(jnp.bfloat16)
    parts = jnp.where(row < count, high.astype(jnp.float32), low.astype(jnp.float32))
    here = lax.broadcasted_iota(jnp.int32, (sessions, sessions), 0)
    there = lax.broadcasted_iota(jnp.int32, (sessions, sessions), 1)
    eye = (here == there).astype(jnp.bfloat16)
    return lax.dot_general(
        eye,
        parts.astype(jnp.bfloat16),
        (((1,), (1,)), ((), ())),
        preferred_element_type=jnp.float32,
    )


def gate_column(table, expert, count):
    lane = lax.broadcasted_iota(jnp.int32, table.shape, 1)
    chosen = (lane == expert) | (lane == expert + count)
    return jnp.sum(jnp.where(chosen, table, 0.0), axis=1, keepdims=True)


def hidden_units(rows, gate_weight, up_weight):
    gate = jnp.dot(rows, gate_weight, preferred_element_type=jnp.float32)
    up = jnp.dot(rows, up_weight, preferred_element_type=jnp.float32)
    return (jax.nn.silu(gate) * up).astype(jnp.bfloat16)


def kernel(
    n,
    m,
    tokens,
    gain,
    ids,
    gates,
    w_gate,
    w_up,
    w_down,
    talker_in,
    talker_gain,
    talker_ids,
    talker_gates,
    t_gate,
    t_up,
    t_down,
    conv_state,
    conv_kernel,
    conv_gain,
    thought,
    spoken,
    audio,
    new_state,
    held,
    part,
    sib_out,
    sib_in,
    ret_out,
    ret_in,
    total,
    talk_held,
    talk_out,
    talk_in,
    wg,
    wu,
    wd,
    tg,
    tu,
    td,
    state,
    w_sem,
    held_recv,
    up_send,
    down_send,
    side_send,
    sib_send,
    sib_recv,
    ret_send,
    ret_recv,
    talk_send,
    talk_recv,
    back_send,
    back_recv,
):
    me = lax.axis_index("exp")
    ms = lax.axis_index("sess")
    chips = n // CORES
    z = me // CORES
    c = lax.rem(me, CORES)
    sibling = z * CORES + 1 - c
    sessions, depth = tokens.shape
    width = held.shape[2] - depth

    loads = [
        pltpu.make_async_copy(src, dst, w_sem.at[i])
        for i, (src, dst) in enumerate(
            (
                (w_gate.at[0], wg),
                (w_up.at[0], wu),
                (w_down.at[0], wd),
                (t_gate.at[0], tg),
                (t_up.at[0], tu),
                (t_down.at[0], td),
                (conv_state, state),
            )
        )
    ]
    for load in loads:
        load.start()

    barrier = pltpu.get_barrier_semaphore()
    pl.semaphore_signal(barrier, inc=1, device_id={"exp": sibling}, device_id_type=MESH)
    for k in range(1, chips):
        other = lax.rem(z + k, chips) * CORES + c
        pl.semaphore_signal(barrier, inc=1, device_id={"exp": other}, device_id_type=MESH)
    for k in range(1, m):
        pl.semaphore_signal(barrier, inc=1, device_id={"sess": lax.rem(ms + k, m)}, device_id_type=MESH)

    held[me, :, :depth] = rms_scale(tokens[...], gain[...])
    held[me, :, depth:] = gate_table(ids[...], gates[...], n, width).astype(jnp.bfloat16)
    talk_held[ms] = rms_scale(talker_in[...], talker_gain[...])
    pl.semaphore_wait(barrier, chips + m - 1)

    def pass_on(slot, send_sem, target):
        return pltpu.make_async_remote_copy(
            src_ref=held.at[slot],
            dst_ref=held.at[slot],
            send_sem=send_sem,
            recv_sem=held_recv.at[slot],
            device_id={"exp": target},
            device_id_type=MESH,
        )

    def upward(chip):
        return pass_on(chip * CORES + c, up_send.at[chip], lax.rem(me + CORES, n))

    def downward(chip):
        return pass_on(chip * CORES + c, down_send.at[chip], lax.rem(me + n - CORES, n))

    def sideways(chip):
        return pass_on(chip * CORES + c, side_send.at[chip], sibling)

    def talk_copy(source, target, send_sem, recv_sem, peer, k):
        return pltpu.make_async_remote_copy(
            src_ref=source,
            dst_ref=target,
            send_sem=send_sem.at[k],
            recv_sem=recv_sem.at[ms],
            device_id={"sess": peer},
            device_id_type=MESH,
        )

    def arrival(buffer, recv_sem, slot):
        pltpu.make_async_copy(buffer.at[slot], buffer.at[slot], recv_sem.at[slot]).wait()

    def sib_copy(chip):
        return pltpu.make_async_remote_copy(
            src_ref=sib_out.at[chip],
            dst_ref=sib_in.at[chip],
            send_sem=sib_send.at[chip],
            recv_sem=sib_recv.at[chip],
            device_id={"exp": sibling},
            device_id_type=MESH,
        )

    def ret_copy(chip):
        return pltpu.make_async_remote_copy(
            src_ref=ret_out.at[chip],
            dst_ref=ret_in.at[z],
            send_sem=ret_send.at[chip],
            recv_sem=ret_recv.at[z],
            device_id={"exp": chip * CORES + c},
            device_id_type=MESH,
        )

    @pl.when(z + 1 < chips)
    def _():
        upward(z).start()

    @pl.when(z > 0)
    def _():
        downward(z).start()

    sideways(z).start()
    for k in range(1, m):
        talk_copy(talk_held.at[ms], talk_held.at[ms], talk_send, talk_recv, lax.rem(ms + k, m), k).start()

    def compute(chip):
        rows = held[pl.ds(chip * CORES, CORES)].reshape(CORES * sessions, depth + width)
        column = gate_column(rows[:, depth:].astype(jnp.float32), me, n)
        hidden = hidden_units(rows[:, :depth], wg[...], wu[...])
        step = min(512, depth)
        for at in range(0, depth, step):
            out = jnp.dot(hidden, wd[:, at : at + step], preferred_element_type=jnp.float32)
            part[:, :, at : at + step] = (out * column).reshape(CORES, sessions, step)
        sib_out[chip] = part[1 - c].astype(jnp.bfloat16)
        sib_copy(chip).start()

    def order(k):
        both = jnp.minimum(z, chips - 1 - z)
        near = (k + 1) // 2
        paired = jnp.where(lax.rem(k, 2) == 1, z - near, z + near)
        single = jnp.where(z < chips - 1 - z, z + k - both, z - k + both)
        return jnp.where(k <= 2 * both, paired, single)

    for load in loads[:3]:
        load.wait()
    arrival(held, held_recv, sibling)
    compute(z)
    total[...] = tokens[...].astype(jnp.float32) + part[c]

    def step(k, carry):
        chip = order(k)
        arrival(held, held_recv, chip * CORES + c)

        @pl.when((chip < z) & (z + 1 < chips))
        def _():
            upward(chip).start()

        @pl.when((chip > z) & (z > 0))
        def _():
            downward(chip).start()

        sideways(chip).start()
        before = order(k - 1)
        finish(before)
        arrival(held, held_recv, chip * CORES + 1 - c)
        compute(chip)
        ret_out[chip] = part[c].astype(jnp.bfloat16)
        return carry

    def finish(chip):
        arrival(sib_in, sib_recv, chip)

        @pl.when(chip == z)
        def _():
            total[...] = total[...] + sib_in[chip].astype(jnp.float32)

        @pl.when(chip != z)
        def _():
            ret_out[chip] = (ret_out[chip].astype(jnp.float32) + sib_in[chip].astype(jnp.float32)).astype(jnp.bfloat16)
            ret_copy(chip).start()

    lax.fori_loop(1, chips, step, 0)
    finish(order(chips - 1))

    for load in loads[3:6]:
        load.wait()
    for k in range(1, m):
        arrival(talk_held, talk_recv, lax.rem(ms + k, m))
    talk_depth = talker_in.shape[1]
    rows = talk_held[...].reshape(m * sessions, talk_depth)
    hidden = hidden_units(rows, tg[...], tu[...])
    out = jnp.dot(hidden, td[...], preferred_element_type=jnp.float32)
    talk_out[...] = out.astype(jnp.bfloat16).reshape(m, sessions, talk_depth)
    for k in range(1, m):
        peer = lax.rem(ms + k, m)
        talk_copy(talk_out.at[peer], talk_in.at[ms], back_send, back_recv, peer, k).start()
    talk_in[ms] = talk_out[ms]
    table = gate_table(talker_ids[...], talker_gates[...], m, 128 * (-(-2 * m // 128)))
    loads[6].wait()
    for k in range(1, m):
        arrival(talk_in, back_recv, lax.rem(ms + k, m))
    said = talker_in[...].astype(jnp.float32)
    for e in range(m):
        said = said + gate_column(table, e, m) * talk_in[e].astype(jnp.float32)
    said = said.astype(jnp.bfloat16)
    spoken[...] = said
    taps = conv_kernel.shape[0]
    newest = said.astype(jnp.float32)
    mixed = newest * conv_kernel[taps - 1 : taps, :]
    for j in range(taps - 1):
        mixed = mixed + state[j] * conv_kernel[j : j + 1, :]
        if j > 0:
            new_state[j - 1] = state[j]
    new_state[taps - 2] = newest
    scale = lax.rsqrt(jnp.mean(mixed * mixed, axis=-1, keepdims=True) + 1e-06)
    audio[...] = (mixed * scale * conv_gain[...]).astype(jnp.bfloat16)

    for k in range(1, chips):
        chip = order(k)
        arrival(ret_in, ret_recv, chip)
        total[...] = total[...] + ret_in[chip].astype(jnp.float32)
    thought[...] = total[...].astype(jnp.bfloat16)

    @pl.when(z + 1 < chips)
    def _():
        upward(z).wait_send()

    @pl.when(z > 0)
    def _():
        downward(z).wait_send()

    sideways(z).wait_send()
    sib_copy(z).wait_send()
    for k in range(1, chips):
        chip = order(k)

        @pl.when((chip < z) & (z + 1 < chips))
        def _():
            upward(chip).wait_send()

        @pl.when((chip > z) & (z > 0))
        def _():
            downward(chip).wait_send()

        sideways(chip).wait_send()
        sib_copy(chip).wait_send()
        ret_copy(chip).wait_send()
    for k in range(1, m):
        peer = lax.rem(ms + k, m)
        talk_copy(talk_held.at[ms], talk_held.at[ms], talk_send, talk_recv, peer, k).wait_send()
        talk_copy(talk_out.at[peer], talk_in.at[ms], back_send, back_recv, peer, k).wait_send()


def shards(
    tokens,
    thinker_gain,
    thinker_ids,
    thinker_gates,
    w_gate,
    w_up,
    w_down,
    talker_in,
    talker_gain,
    talker_ids,
    talker_gates,
    t_gate,
    t_up,
    t_down,
    conv_state,
    conv_kernel,
    conv_gain,
):
    n = lax.axis_size("exp")
    m = lax.axis_size("sess")
    chips = n // CORES
    sessions, depth = tokens.shape
    talk_depth = talker_in.shape[1]
    width = 128 * (-(-2 * n // 128))
    taps = conv_kernel.shape[0]
    half = jnp.bfloat16
    vmem = pl.BlockSpec(memory_space=pltpu.VMEM)
    hbm = pl.BlockSpec(memory_space=pl.ANY)
    dma = pltpu.SemaphoreType.DMA
    thought, spoken, audio, new_state = pl.pallas_call(
        functools.partial(kernel, n, m),
        out_shape=(
            jax.ShapeDtypeStruct((sessions, depth), half),
            jax.ShapeDtypeStruct((sessions, talk_depth), half),
            jax.ShapeDtypeStruct((sessions, talk_depth), half),
            jax.ShapeDtypeStruct((taps - 1, sessions, talk_depth), jnp.float32),
        ),
        in_specs=[vmem, vmem, vmem, vmem, hbm, hbm, hbm, vmem, vmem, vmem, vmem, hbm, hbm, hbm, hbm, vmem, vmem],
        out_specs=(vmem, vmem, vmem, vmem),
        scratch_shapes=[
            pltpu.VMEM((n, sessions, depth + width), half),
            pltpu.VMEM((CORES, sessions, depth), jnp.float32),
            pltpu.VMEM((chips, sessions, depth), half),
            pltpu.VMEM((chips, sessions, depth), half),
            pltpu.VMEM((chips, sessions, depth), half),
            pltpu.VMEM((chips, sessions, depth), half),
            pltpu.VMEM((sessions, depth), jnp.float32),
            pltpu.VMEM((m, sessions, talk_depth), half),
            pltpu.VMEM((m, sessions, talk_depth), half),
            pltpu.VMEM((m, sessions, talk_depth), half),
            pltpu.VMEM(w_gate.shape[1:], half),
            pltpu.VMEM(w_up.shape[1:], half),
            pltpu.VMEM(w_down.shape[1:], half),
            pltpu.VMEM(t_gate.shape[1:], half),
            pltpu.VMEM(t_up.shape[1:], half),
            pltpu.VMEM(t_down.shape[1:], half),
            pltpu.VMEM((taps - 1, sessions, talk_depth), jnp.float32),
            dma((7,)),
            dma((n,)),
            dma((chips,)),
            dma((chips,)),
            dma((chips,)),
            dma((chips,)),
            dma((chips,)),
            dma((chips,)),
            dma((chips,)),
            dma((m,)),
            dma((m,)),
            dma((m,)),
            dma((m,)),
        ],
        compiler_params=pltpu.CompilerParams(
            collective_id=0, has_side_effects=True, vmem_limit_bytes=48 * 1024 * 1024
        ),
    )(
        tokens,
        thinker_gain[None],
        thinker_ids.T,
        thinker_gates.T,
        w_gate,
        w_up,
        w_down,
        talker_in,
        talker_gain[None],
        talker_ids.T,
        talker_gates.T,
        t_gate,
        t_up,
        t_down,
        jnp.transpose(conv_state, (1, 0, 2)),
        conv_kernel,
        conv_gain[None],
    )
    return thought, spoken, audio, jnp.transpose(new_state, (1, 0, 2))


def solution(mesh):
    placed = (
        P(("sess", "exp"), None),
        P(),
        P(("sess", "exp"), None),
        P(("sess", "exp"), None),
        P("exp", None, None),
        P("exp", None, None),
        P("exp", None, None),
        P(("sess", "exp"), None),
        P(),
        P(("sess", "exp"), None),
        P(("sess", "exp"), None),
        P("sess", None, None),
        P("sess", None, None),
        P("sess", None, None),
        P(("sess", "exp"), None, None),
        P(),
        P(),
    )
    return jax.shard_map(
        shards,
        mesh=mesh,
        in_specs=placed,
        out_specs=(
            P(("sess", "exp"), None),
            P(("sess", "exp"), None),
            P(("sess", "exp"), None),
            P(("sess", "exp"), None, None),
        ),
        check_vma=False,
    )
```

time: 103 us -> 51.4 us (0.50)
  waiting for transfers between devices: 40.6 us -> 0 us
  Pallas kernels: 0 us -> 35.8 us
  matrix products: 18.8 us -> 0 us
  starting transfers between devices: 18.6 us -> 0 us
  other arithmetic: 15.1 us -> 0 us
  local copies, waits for them, and re-layouts: 8.17 us -> 14.3 us
    all_to_all x4 -> x0, waiting for transfers between devices: 40.6 us -> none  [the longest x1 21.2 us: shards(): lax.all_to_all(buckets, 'exp', split_axis=0, concat_axis=0, tiled=True)]
    pallas_call x0 -> x1, Pallas kernels: none -> 35.8 us  [shards(): pl.pallas_call(functools.partial(kernel, n, m), out_shape=(jax.ShapeDtype...]
    dot_general x6 -> x0, matrix products: 18.8 us -> none  [the longest x2 8.31 us: expert_rows(): jnp.dot(hidden, weight_down, preferred_element_type=jnp.float32)]
    all_to_all x4 -> x0, starting transfers between devices: 18.6 us -> none  [the longest x1 5.16 us: shards(): lax.all_to_all(buckets, 'sess', split_axis=0, concat_axis=0, tiled=True)]
    unnamed x16 -> x32, local copies, waits for them, and re-layouts: 0.2 us -> 14.3 us
    reduce_sum x10 -> x0, other arithmetic: 9.53 us -> none  [the longest x2 3.4 us: combine_back(): total = jnp.sum(gates[:, :, None] * picked.astype(jnp.float32), axis=1)]
    gather x3 -> x0, local copies, waits for them, and re-layouts: 7.11 us -> none  [combine_back(): jnp.take(flat, places.reshape(-1), axis=0)]
    concatenate x1 -> x0, other arithmetic: 1.73 us -> none  [shards(): jnp.concatenate([conv_state, spoken.astype(jnp.float32)[:, None, :]], axi...]
  transfers between devices with their start and end apart: 4 -> 0, of which waited for: 2 -> 0; matrix products, arithmetic and copies ran while one was open for 28% -> 0% of each run, Pallas kernels for 0% -> 0%
where the time goes in v1:
time: 51.4 us; the launch traced here: 50.8 us
  Pallas kernels  35.8 us (70%)
  local copies, waits for them, and re-layouts  14.3 us (28%)
  between operations  0.67 us (1%)
    pallas_call x1, Pallas kernels, shards(): pl.pallas_call(functools.partial(kernel, n, m), out_shape=(jax.ShapeDtype...  35.8 us
    unnamed x32, local copies, waits for them, and re-layouts  14.3 us

profile of v1, /device:TPU:0, one launch (start us, length us, event | category | flops | bytes accessed | tf_op | source)
XLA Modules:
  0.0 50.8 jit_solution(10782864435476484952)
XLA Ops:
  0.6 0.0 copy-start
  0.6 1.1 %copy-done = bf16[1,1024,384]{2,1,0:T(8,128)(2,1)S(1)} copy-done((bf16[1,1024,384]{2,1,0:T(8,128)(2,1)S(1)}, bf16[1,1024,384]{2,1,0:T(8,128)(2,1)}, u32[]{:S(2)}) %copy-start) | copy-done | bytes 786456
  1.8 0.0 copy-start.1
  1.8 1.1 %copy-done.1 = bf16[1,1024,384]{2,1,0:T(8,128)(2,1)S(1)} copy-done((bf16[1,1024,384]{2,1,0:T(8,128)(2,1)S(1)}, bf16[1,1024,384]{2,1,0:T(8,128)(2,1)}, u32[]{:S(2)}) %copy-start.1) | copy-done | bytes 786456
  2.9 0.0 copy-start.2
  2.9 1.1 %copy-done.2 = bf16[1,384,1024]{2,1,0:T(8,128)(2,1)S(1)} copy-done((bf16[1,384,1024]{2,1,0:T(8,128)(2,1)S(1)}, bf16[1,384,1024]{2,1,0:T(8,128)(2,1)}, u32[]{:S(2)}) %copy-start.2) | copy-done | bytes 786456
  4.0 0.0 copy-start.3
  4.0 1.0 %copy-done.3 = f32[32,3,1024]{2,0,1:T(8,128)S(1)} copy-done((f32[32,3,1024]{2,0,1:T(8,128)S(1)}, f32[32,3,1024]{2,0,1:T(8,128)}, u32[]{:S(2)}) %copy-start.3) | copy-done | bytes 393240
  5.0 0.0 copy-start.4
  5.0 0.9 %copy-done.4 = bf16[32,2048]{1,0:T(8,128)(2,1)S(1)} copy-done((bf16[32,2048]{1,0:T(8,128)(2,1)S(1)}, bf16[32,2048]{1,0:T(8,128)(2,1)}, u32[]{:S(2)}) %copy-start.4) | copy-done | bytes 131096
  5.9 0.8 %copy-done.5 = bf16[32,1024]{1,0:T(8,128)(2,1)S(1)} copy-done((bf16[32,1024]{1,0:T(8,128)(2,1)S(1)}, bf16[32,1024]{1,0:T(8,128)(2,1)}, u32[]{:S(2)}) %copy-start.5) | copy-done | bytes 65560
  6.8 0.7 %copy-done.6 = f32[4,1024]{1,0:T(4,128)S(1)} copy-done((f32[4,1024]{1,0:T(4,128)S(1)}, f32[4,1024]{1,0:T(4,128)}, u32[]{:S(2)}) %copy-start.6) | copy-done | bytes 16408
  7.5 0.7 %copy-done.7 = f32[2048]{0:T(1024)S(1)} copy-done((f32[2048]{0:T(1024)S(1)}, f32[2048]{0:T(1024)}, u32[]{:S(2)}) %copy-start.7) | copy-done | bytes 8216
  8.2 0.7 %copy-done.8 = s32[32,8]{0,1:T(8,128)S(1)} copy-done((s32[32,8]{0,1:T(8,128)S(1)}, s32[32,8]{0,1:T(8,128)}, u32[]{:S(2)}) %copy-start.8) | copy-done | bytes 1048
  8.9 0.7 %copy-done.9 = f32[32,8]{0,1:T(8,128)S(1)} copy-done((f32[32,8]{0,1:T(8,128)S(1)}, f32[32,8]{0,1:T(8,128)}, u32[]{:S(2)}) %copy-start.9) | copy-done | bytes 1048
  9.6 0.7 %copy-done.10 = f32[1024]{0:T(1024)S(1)} copy-done((f32[1024]{0:T(1024)S(1)}, f32[1024]{0:T(1024)}, u32[]{:S(2)}) %copy-start.10) | copy-done | bytes 4120
  10.3 0.7 %copy-done.11 = f32[1024]{0:T(1024)S(1)} copy-done((f32[1024]{0:T(1024)S(1)}, f32[1024]{0:T(1024)}, u32[]{:S(2)}) %copy-start.11) | copy-done | bytes 4120
  10.9 0.7 %copy-done.12 = s32[32,2]{0,1:T(2,128)S(1)} copy-done((s32[32,2]{0,1:T(2,128)S(1)}, s32[32,2]{0,1:T(2,128)}, u32[]{:S(2)}) %copy-start.12) | copy-done | bytes 280
  11.6 0.7 %copy-done.13 = f32[32,2]{0,1:T(2,128)S(1)} copy-done((f32[32,2]{0,1:T(2,128)S(1)}, f32[32,2]{0,1:T(2,128)}, u32[]{:S(2)}) %copy-start.13) | copy-done | bytes 280
  12.3 35.8 %shard_map.192 = (bf16[32,2048]{1,0:T(8,128)(2,1)S(1)}, bf16[32,1024]{1,0:T(8,128)(2,1)S(1)}, bf16[32,1024]{1,0:T(8,128)(2,1)S(1)}, f32[3,32,1024]{2,1,0:T(8,128)S(1)}) custom-call(bf16[32,2048]{1,0:T(8,128)(2,1)S(1)} %copy-done.4, f32[1,2048]{1,0:T(1,128)S(1)} %bitcast.11, s32[8,32]{1,0:T(8,128)S(1)} %bitcast.12, f32[8,32]{1,0:T(8,128)S(1)} %bitcast.13, ...), custom_call_target="tpu_custom_call" | custom-call | tf_op jit(solution)/shard_map/pallas_call | solution.py:370
  48.1 0.7 %copy.25 = bf16[32,2048]{1,0:T(8,128)(2,1)} copy(bf16[32,2048]{1,0:T(8,128)(2,1)S(1)} %get-tuple-element.16) | data formatting | bytes 262144
  48.8 0.6 %copy.26 = bf16[32,1024]{1,0:T(8,128)(2,1)} copy(bf16[32,1024]{1,0:T(8,128)(2,1)S(1)} %get-tuple-element.17) | data formatting | bytes 131072
  49.4 0.6 %copy.27 = bf16[32,1024]{1,0:T(8,128)(2,1)} copy(bf16[32,1024]{1,0:T(8,128)(2,1)S(1)} %get-tuple-element.18) | data formatting | bytes 131072
  50.1 0.7 %copy.28 = f32[32,3,1024]{2,0,1:T(8,128)} copy(f32[32,3,1024]{2,0,1:T(8,128)S(1)} %bitcast.10) | data formatting | bytes 786432
  (9 shorter events, 0.0 us)
Async XLA Ops:
  0.6 1.1 %copy-start = (bf16[1,1024,384]{2,1,0:T(8,128)(2,1)S(1)}, bf16[1,1024,384]{2,1,0:T(8,128)(2,1)}, u32[]{:S(2)}) copy-start(bf16[1,1024,384]{2,1,0:T(8,128)(2,1)} %t_gate.1) | copy-start | bytes 2359300
  1.8 1.1 %copy-start.1 = (bf16[1,1024,384]{2,1,0:T(8,128)(2,1)S(1)}, bf16[1,1024,384]{2,1,0:T(8,128)(2,1)}, u32[]{:S(2)}) copy-start(bf16[1,1024,384]{2,1,0:T(8,128)(2,1)} %t_up.1) | copy-start | bytes 2359300
  2.9 1.1 %copy-start.2 = (bf16[1,384,1024]{2,1,0:T(8,128)(2,1)S(1)}, bf16[1,384,1024]{2,1,0:T(8,128)(2,1)}, u32[]{:S(2)}) copy-start(bf16[1,384,1024]{2,1,0:T(8,128)(2,1)} %t_down.1) | copy-start | bytes 2359300
  4.0 1.0 %copy-start.3 = (f32[32,3,1024]{2,0,1:T(8,128)S(1)}, f32[32,3,1024]{2,0,1:T(8,128)}, u32[]{:S(2)}) copy-start(f32[32,3,1024]{2,0,1:T(8,128)} %param.31) | copy-start | bytes 1179652
  5.0 0.9 %copy-start.4 = (bf16[32,2048]{1,0:T(8,128)(2,1)S(1)}, bf16[32,2048]{1,0:T(8,128)(2,1)}, u32[]{:S(2)}) copy-start(bf16[32,2048]{1,0:T(8,128)(2,1)} %tokens.1) | copy-start | bytes 393220
  5.9 0.8 %copy-start.5 = (bf16[32,1024]{1,0:T(8,128)(2,1)S(1)}, bf16[32,1024]{1,0:T(8,128)(2,1)}, u32[]{:S(2)}) copy-start(bf16[32,1024]{1,0:T(8,128)(2,1)} %talker_in.1) | copy-start | bytes 196612
  6.8 0.7 %copy-start.6 = (f32[4,1024]{1,0:T(4,128)S(1)}, f32[4,1024]{1,0:T(4,128)}, u32[]{:S(2)}) copy-start(f32[4,1024]{1,0:T(4,128)} %conv_kernel.1) | copy-start | bytes 49156
  7.5 0.7 %copy-start.7 = (f32[2048]{0:T(1024)S(1)}, f32[2048]{0:T(1024)}, u32[]{:S(2)}) copy-start(f32[2048]{0:T(1024)} %param.18) | copy-start | bytes 24580
  8.2 0.7 %copy-start.8 = (s32[32,8]{0,1:T(8,128)S(1)}, s32[32,8]{0,1:T(8,128)}, u32[]{:S(2)}) copy-start(s32[32,8]{0,1:T(8,128)} %param.19) | copy-start | bytes 3076
  8.9 0.7 %copy-start.9 = (f32[32,8]{0,1:T(8,128)S(1)}, f32[32,8]{0,1:T(8,128)}, u32[]{:S(2)}) copy-start(f32[32,8]{0,1:T(8,128)} %param.20) | copy-start | bytes 3076
  9.6 0.7 %copy-start.10 = (f32[1024]{0:T(1024)S(1)}, f32[1024]{0:T(1024)}, u32[]{:S(2)}) copy-start(f32[1024]{0:T(1024)} %param.25) | copy-start | bytes 12292
  10.3 0.7 %copy-start.11 = (f32[1024]{0:T(1024)S(1)}, f32[1024]{0:T(1024)}, u32[]{:S(2)}) copy-start(f32[1024]{0:T(1024)} %param.33) | copy-start | bytes 12292
  10.9 0.7 %copy-start.12 = (s32[32,2]{0,1:T(2,128)S(1)}, s32[32,2]{0,1:T(2,128)}, u32[]{:S(2)}) copy-start(s32[32,2]{0,1:T(2,128)} %param.26) | copy-start | bytes 772
  11.6 0.7 %copy-start.13 = (f32[32,2]{0,1:T(2,128)S(1)}, f32[32,2]{0,1:T(2,128)}, u32[]{:S(2)}) copy-start(f32[32,2]{0,1:T(2,128)} %param.27) | copy-start | bytes 772

commit v2 on v1

--- a/solution.py
+++ b/solution.py
@@ -9,6 +9,7 @@
 
 MESH = pl.DeviceIdType.MESH
 CORES = 2
+VMEM = 64 * 1024 * 1024
 
 
 def rms_scale(values, gain):
@@ -51,61 +52,16 @@
     return (jax.nn.silu(gate) * up).astype(jnp.bfloat16)
 
 
-def kernel(
-    n,
-    m,
-    tokens,
-    gain,
-    ids,
-    gates,
-    w_gate,
-    w_up,
-    w_down,
-    talker_in,
-    talker_gain,
-    talker_ids,
-    talker_gates,
-    t_gate,
-    t_up,
-    t_down,
-    conv_state,
-    conv_kernel,
-    conv_gain,
-    thought,
-    spoken,
-    audio,
-    new_state,
-    held,
-    part,
-    sib_out,
-    sib_in,
-    ret_out,
-    ret_in,
-    total,
-    talk_held,
-    talk_out,
-    talk_in,
-    wg,
-    wu,
-    wd,
-    tg,
-    tu,
-    td,
-    state,
-    w_sem,
-    held_recv,
-    up_send,
-    down_send,
-    side_send,
-    sib_send,
-    sib_recv,
-    ret_send,
-    ret_recv,
-    talk_send,
-    talk_recv,
-    back_send,
-    back_recv,
-):
+def kernel(n, m, *refs):
+    inputs, refs = refs[:17], refs[17:]
+    results, refs = refs[:4], refs[4:]
+    (thought, spoken, audio, new_state), out_sem, refs = refs[:4], refs[4], refs[5:]
+    local, in_sem, refs = refs[:17], refs[17], refs[18:]
+    (held, part, sib_out, sib_in, ret_out, ret_in, total, talk_held, talk_out, talk_in), refs = refs[:10], refs[10:]
+    (held_recv, up_send, down_send, side_send, sib_send, sib_recv, ret_send, ret_recv), refs = refs[:8], refs[8:]
+    talk_send, talk_recv, back_send, back_recv = refs
+    (tokens, gain, ids, gates, wg, wu, wd, talker_in, talker_gain) = local[:9]
+    (talker_ids, talker_gates, tg, tu, td, state, conv_kernel, conv_gain) = local[9:]
     me = lax.axis_index("exp")
     ms = lax.axis_index("sess")
     chips = n // CORES
@@ -115,22 +71,9 @@
     sessions, depth = tokens.shape
     width = held.shape[2] - depth
 
-    loads = [
-        pltpu.make_async_copy(src, dst, w_sem.at[i])
-        for i, (src, dst) in enumerate(
-            (
-                (w_gate.at[0], wg),
-                (w_up.at[0], wu),
-                (w_down.at[0], wd),
-                (t_gate.at[0], tg),
-                (t_up.at[0], tu),
-                (t_down.at[0], td),
-                (conv_state, state),
-            )
-        )
-    ]
-    for load in loads:
-        load.start()
+    loads = [pltpu.make_async_copy(inputs[i], local[i], in_sem.at[i]) for i in range(17)]
+    for i in (0, 1, 2, 3, 7, 8, 4, 5, 6, 11, 12, 13, 9, 10, 15, 16, 14):
+        loads[i].start()
 
     barrier = pltpu.get_barrier_semaphore()
     pl.semaphore_signal(barrier, inc=1, device_id={"exp": sibling}, device_id_type=MESH)
@@ -140,8 +83,12 @@
     for k in range(1, m):
         pl.semaphore_signal(barrier, inc=1, device_id={"sess": lax.rem(ms + k, m)}, device_id_type=MESH)
 
+    for i in (0, 1, 2, 3):
+        loads[i].wait()
     held[me, :, :depth] = rms_scale(tokens[...], gain[...])
     held[me, :, depth:] = gate_table(ids[...], gates[...], n, width).astype(jnp.bfloat16)
+    for i in (7, 8):
+        loads[i].wait()
     talk_held[ms] = rms_scale(talker_in[...], talker_gain[...])
     pl.semaphore_wait(barrier, chips + m - 1)
 
@@ -220,56 +167,47 @@
         sib_out[chip] = part[1 - c].astype(jnp.bfloat16)
         sib_copy(chip).start()
 
-    def order(k):
-        both = jnp.minimum(z, chips - 1 - z)
-        near = (k + 1) // 2
-        paired = jnp.where(lax.rem(k, 2) == 1, z - near, z + near)
-        single = jnp.where(z < chips - 1 - z, z + k - both, z - k + both)
-        return jnp.where(k <= 2 * both, paired, single)
-
-    for load in loads[:3]:
-        load.wait()
+    toward = jnp.where(2 * z < chips, 1, -1)
+
+    def valid(chip):
+        return (chip >= 0) & (chip < chips)
+
+    def forward(s):
+        for side in (1, -1):
+            chip = z + toward * side * s
+
+            @pl.when(valid(chip))
+            def _():
+                arrival(held, held_recv, chip * CORES + c)
+
+                @pl.when((chip < z) & (z + 1 < chips))
+                def _():
+                    upward(chip).start()
+
+                @pl.when((chip > z) & (z > 0))
+                def _():
+                    downward(chip).start()
+
+                sideways(chip).start()
+
+    def finish(chip):
+        arrival(sib_in, sib_recv, chip)
+        ret_out[chip] = (part[c] + sib_in[chip].astype(jnp.float32)).astype(jnp.bfloat16)
+        ret_copy(chip).start()
+
+    def unit(chip):
+        arrival(held, held_recv, chip * CORES + 1 - c)
+        compute(chip)
+
+    for i in (4, 5, 6):
+        loads[i].wait()
     arrival(held, held_recv, sibling)
     compute(z)
     total[...] = tokens[...].astype(jnp.float32) + part[c]
-
-    def step(k, carry):
-        chip = order(k)
-        arrival(held, held_recv, chip * CORES + c)
-
-        @pl.when((chip < z) & (z + 1 < chips))
-        def _():
-            upward(chip).start()
-
-        @pl.when((chip > z) & (z > 0))
-        def _():
-            downward(chip).start()
-
-        sideways(chip).start()
-        before = order(k - 1)
-        finish(before)
-        arrival(held, held_recv, chip * CORES + 1 - c)
-        compute(chip)
-        ret_out[chip] = part[c].astype(jnp.bfloat16)
-        return carry
-
-    def finish(chip):
-        arrival(sib_in, sib_recv, chip)
-
-        @pl.when(chip == z)
-        def _():
-            total[...] = total[...] + sib_in[chip].astype(jnp.float32)
-
-        @pl.when(chip != z)
-        def _():
-            ret_out[chip] = (ret_out[chip].astype(jnp.float32) + sib_in[chip].astype(jnp.float32)).astype(jnp.bfloat16)
-            ret_copy(chip).start()
-
-    lax.fori_loop(1, chips, step, 0)
-    finish(order(chips - 1))
-
-    for load in loads[3:6]:
-        load.wait()
+    forward(1)
+
+    for i in (11, 12, 13):
+        loads[i].wait()
     for k in range(1, m):
         arrival(talk_held, talk_recv, lax.rem(ms + k, m))
     talk_depth = talker_in.shape[1]
@@ -280,9 +218,38 @@
     for k in range(1, m):
         peer = lax.rem(ms + k, m)
         talk_copy(talk_out.at[peer], talk_in.at[ms], back_send, back_recv, peer, k).start()
+
+    def level(s, carry):
+        first = z + toward * s
+        second = z - toward * s
+
+        @pl.when(valid(first))
+        def _():
+            unit(first)
+
+        @pl.when(s + 1 < chips)
+        def _():
+            forward(s + 1)
+
+        @pl.when(valid(first))
+        def _():
+            finish(first)
+
+        @pl.when(valid(second))
+        def _():
+            unit(second)
+            finish(second)
+
+        return carry
+
+    lax.fori_loop(1, chips, level, 0)
+    arrival(sib_in, sib_recv, z)
+    total[...] = total[...] + sib_in[z].astype(jnp.float32)
+
+    for i in (9, 10, 14, 15, 16):
+        loads[i].wait()
     talk_in[ms] = talk_out[ms]
     table = gate_table(talker_ids[...], talker_gates[...], m, 128 * (-(-2 * m // 128)))
-    loads[6].wait()
     for k in range(1, m):
         arrival(talk_in, back_recv, lax.rem(ms + k, m))
     said = talker_in[...].astype(jnp.float32)
@@ -300,12 +267,17 @@
     new_state[taps - 2] = newest
     scale = lax.rsqrt(jnp.mean(mixed * mixed, axis=-1, keepdims=True) + 1e-06)
     audio[...] = (mixed * scale * conv_gain[...]).astype(jnp.bfloat16)
+    staged = (thought, spoken, audio, new_state)
+    writes = [pltpu.make_async_copy(staged[i], results[i], out_sem.at[i]) for i in range(4)]
+    for write in writes[1:]:
+        write.start()
 
     for k in range(1, chips):
-        chip = order(k)
+        chip = lax.rem(z + k, chips)
         arrival(ret_in, ret_recv, chip)
         total[...] = total[...] + ret_in[chip].astype(jnp.float32)
     thought[...] = total[...].astype(jnp.bfloat16)
+    writes[0].start()
 
     @pl.when(z + 1 < chips)
     def _():
@@ -318,7 +290,7 @@
     sideways(z).wait_send()
     sib_copy(z).wait_send()
     for k in range(1, chips):
-        chip = order(k)
+        chip = lax.rem(z + k, chips)
 
         @pl.when((chip < z) & (z + 1 < chips))
         def _():
@@ -335,6 +307,17 @@
         peer = lax.rem(ms + k, m)
         talk_copy(talk_held.at[ms], talk_held.at[ms], talk_send, talk_recv, peer, k).wait_send()
         talk_copy(talk_out.at[peer], talk_in.at[ms], back_send, back_recv, peer, k).wait_send()
+    for write in writes:
+        write.wait()
+
+
+def write_out(*refs):
+    count = len(refs) // 2
+    copies = [pltpu.make_async_copy(refs[i], refs[count + i], refs[-1].at[i]) for i in range(count)]
+    for copy in copies:
+        copy.start()
+    for copy in copies:
+        copy.wait()
 
 
 def shards(
@@ -364,20 +347,43 @@
     width = 128 * (-(-2 * n // 128))
     taps = conv_kernel.shape[0]
     half = jnp.bfloat16
-    vmem = pl.BlockSpec(memory_space=pltpu.VMEM)
-    hbm = pl.BlockSpec(memory_space=pl.ANY)
+    hbm = pl.BlockSpec(memory_space=pltpu.HBM)
     dma = pltpu.SemaphoreType.DMA
-    thought, spoken, audio, new_state = pl.pallas_call(
+    operands = (
+        tokens,
+        thinker_gain[None],
+        thinker_ids.T,
+        thinker_gates.T,
+        w_gate[0],
+        w_up[0],
+        w_down[0],
+        talker_in,
+        talker_gain[None],
+        talker_ids.T,
+        talker_gates.T,
+        t_gate[0],
+        t_up[0],
+        t_down[0],
+        jnp.transpose(conv_state, (1, 0, 2)),
+        conv_kernel,
+        conv_gain[None],
+    )
+    shapes = (
+        jax.ShapeDtypeStruct((sessions, depth), half),
+        jax.ShapeDtypeStruct((sessions, talk_depth), half),
+        jax.ShapeDtypeStruct((sessions, talk_depth), half),
+        jax.ShapeDtypeStruct((taps - 1, sessions, talk_depth), jnp.float32),
+    )
+    results = pl.pallas_call(
         functools.partial(kernel, n, m),
-        out_shape=(
-            jax.ShapeDtypeStruct((sessions, depth), half),
-            jax.ShapeDtypeStruct((sessions, talk_depth), half),
-            jax.ShapeDtypeStruct((sessions, talk_depth), half),
-            jax.ShapeDtypeStruct((taps - 1, sessions, talk_depth), jnp.float32),
-        ),
-        in_specs=[vmem, vmem, vmem, vmem, hbm, hbm, hbm, vmem, vmem, vmem, vmem, hbm, hbm, hbm, hbm, vmem, vmem],
-        out_specs=(vmem, vmem, vmem, vmem),
-        scratch_shapes=[
+        out_shape=shapes,
+        in_specs=[hbm] * len(operands),
+        out_specs=tuple(hbm for _ in shapes),
+        scratch_shapes=[pltpu.VMEM(x.shape, x.dtype) for x in shapes]
+        + [dma((len(shapes),))]
+        + [pltpu.VMEM(x.shape, x.dtype) for x in operands]
+        + [
+            dma((len(operands),)),
             pltpu.VMEM((n, sessions, depth + width), half),
             pltpu.VMEM((CORES, sessions, depth), jnp.float32),
             pltpu.VMEM((chips, sessions, depth), half),
@@ -388,14 +394,6 @@
             pltpu.VMEM((m, sessions, talk_depth), half),
             pltpu.VMEM((m, sessions, talk_depth), half),
             pltpu.VMEM((m, sessions, talk_depth), half),
-            pltpu.VMEM(w_gate.shape[1:], half),
-            pltpu.VMEM(w_up.shape[1:], half),
-            pltpu.VMEM(w_down.shape[1:], half),
-            pltpu.VMEM(t_gate.shape[1:], half),
-            pltpu.VMEM(t_up.shape[1:], half),
-            pltpu.VMEM(t_down.shape[1:], half),
-            pltpu.VMEM((taps - 1, sessions, talk_depth), jnp.float32),
-            dma((7,)),
             dma((n,)),
             dma((chips,)),
             dma((chips,)),
@@ -410,27 +408,17 @@
             dma((m,)),
         ],
         compiler_params=pltpu.CompilerParams(
-            collective_id=0, has_side_effects=True, vmem_limit_bytes=48 * 1024 * 1024
+            collective_id=0, has_side_effects=True, vmem_limit_bytes=VMEM
         ),
-    )(
-        tokens,
-        thinker_gain[None],
-        thinker_ids.T,
-        thinker_gates.T,
-        w_gate,
-        w_up,
-        w_down,
-        talker_in,
-        talker_gain[None],
-        talker_ids.T,
-        talker_gates.T,
-        t_gate,
-        t_up,
-        t_down,
-        jnp.transpose(conv_state, (1, 0, 2)),
-        conv_kernel,
-        conv_gain[None],
-    )
+    )(*operands)
+    thought, spoken, audio, new_state = pl.pallas_call(
+        write_out,
+        out_shape=shapes,
+        in_specs=[hbm] * len(shapes),
+        out_specs=tuple(hbm for _ in shapes),
+        scratch_shapes=[dma((len(shapes),))],
+        compiler_params=pltpu.CompilerParams(vmem_limit_bytes=VMEM),
+    )(*results)
     return thought, spoken, audio, jnp.transpose(new_state, (1, 0, 2))
 
 

time: 51.4 us -> 51.3 us (level)
  Pallas kernels: 35.8 us -> 50.5 us
  local copies, waits for them, and re-layouts: 14.3 us -> 0 us
    pallas_call x1 -> x2, Pallas kernels: 35.8 us -> 50.5 us  [the longest x1 29.5 us: shards(): pl.pallas_call(functools.partial(kernel, n, m), out_shape=shapes, in_spec...]
    unnamed x32 -> x0, local copies, waits for them, and re-layouts: 14.3 us -> none
where the time goes in v2:
time: 51.3 us; the launch traced here: 51.1 us
  Pallas kernels  50.5 us (98%)
  between operations  0.65 us (1%)
    pallas_call x1, Pallas kernels, shards(): pl.pallas_call(functools.partial(kernel, n, m), out_shape=shapes, in_spec...  29.5 us
    pallas_call x1, Pallas kernels, shards(): pl.pallas_call(write_out, out_shape=shapes, in_specs=[hbm] * len(shapes),...  21 us

profile of v2, /device:TPU:0, one launch (start us, length us, event | category | flops | bytes accessed | tf_op | source)
XLA Modules:
  0.0 51.1 jit_solution(13801638799264535602)
XLA Ops:
  0.6 29.5 %shard_map.192 = (bf16[32,2048]{1,0:T(8,128)(2,1)}, bf16[32,1024]{1,0:T(8,128)(2,1)}, bf16[32,1024]{1,0:T(8,128)(2,1)}, f32[3,32,1024]{2,1,0:T(8,128)}) custom-call(bf16[32,2048]{1,0:T(8,128)(2,1)} %refs_0_.1, f32[1,2048]{1,0:T(1,128)} %bitcast.22, s32[8,32]{1,0:T(8,128)} %bitcast.23, f32[8,32]{1,0:T(8,128)} %bitcast.24, bf16[2048,768]{1,0:T(8,128)(2,1)} %bitcast.15, ...), custom_call_target="tpu_custom_call" | custom-call | tf_op jit(solution)/shard_map/pallas_call | solution.py:377
  30.2 21.0 %shard_map.193 = (bf16[32,2048]{1,0:T(8,128)(2,1)}, bf16[32,1024]{1,0:T(8,128)(2,1)}, bf16[32,1024]{1,0:T(8,128)(2,1)}, f32[3,32,1024]{2,1,0:T(8,128)}) custom-call(bf16[32,2048]{1,0:T(8,128)(2,1)} %get-tuple-element.12.refs_0_, bf16[32,1024]{1,0:T(8,128)(2,1)} %get-tuple-element.13.refs_1_, bf16[32,1024]{1,0:T(8,128)(2,1)} %get-tuple-element.14.refs_2_, ...), custom_call_target="tpu_custom_call" | custom-call | tf_op jit(solution)/shard_map/pallas_call | solution.py:414

commit v3 on v2

--- a/solution.py
+++ b/solution.py
@@ -156,55 +156,40 @@
     for k in range(1, m):
         talk_copy(talk_held.at[ms], talk_held.at[ms], talk_send, talk_recv, lax.rem(ms + k, m), k).start()
 
-    def compute(chip):
-        rows = held[pl.ds(chip * CORES, CORES)].reshape(CORES * sessions, depth + width)
-        column = gate_column(rows[:, depth:].astype(jnp.float32), me, n)
-        hidden = hidden_units(rows[:, :depth], wg[...], wu[...])
-        step = min(512, depth)
-        for at in range(0, depth, step):
-            out = jnp.dot(hidden, wd[:, at : at + step], preferred_element_type=jnp.float32)
-            part[:, :, at : at + step] = (out * column).reshape(CORES, sessions, step)
-        sib_out[chip] = part[1 - c].astype(jnp.bfloat16)
-        sib_copy(chip).start()
-
-    toward = jnp.where(2 * z < chips, 1, -1)
-
-    def valid(chip):
-        return (chip >= 0) & (chip < chips)
-
-    def forward(s):
-        for side in (1, -1):
-            chip = z + toward * side * s
-
-            @pl.when(valid(chip))
-            def _():
-                arrival(held, held_recv, chip * CORES + c)
-
-                @pl.when((chip < z) & (z + 1 < chips))
-                def _():
-                    upward(chip).start()
-
-                @pl.when((chip > z) & (z > 0))
-                def _():
-                    downward(chip).start()
-
-                sideways(chip).start()
-
-    def finish(chip):
+    both = jnp.minimum(z, chips - 1 - z)
+    middle = both > 0
+
+    def order(k):
+        near = (k + 1) // 2
+        paired = jnp.where(lax.rem(k, 2) == 1, z - near, z + near)
+        single = jnp.where(z < chips - 1 - z, z + k - both, z - k + both)
+        return jnp.where(k <= 2 * both, paired, single)
+
+    def forward(k):
+        chip = order(k)
+        arrival(held, held_recv, chip * CORES + c)
+
+        @pl.when((chip < z) & (z + 1 < chips))
+        def _():
+            upward(chip).start()
+
+        @pl.when((chip > z) & (z > 0))
+        def _():
+            downward(chip).start()
+
+        sideways(chip).start()
+
+    def finish(chip, at):
         arrival(sib_in, sib_recv, chip)
-        ret_out[chip] = (part[c] + sib_in[chip].astype(jnp.float32)).astype(jnp.bfloat16)
+        mine = part[at * CORES + c]
+        ret_out[chip] = (mine + sib_in[chip].astype(jnp.float32)).astype(jnp.bfloat16)
         ret_copy(chip).start()
 
-    def unit(chip):
-        arrival(held, held_recv, chip * CORES + 1 - c)
-        compute(chip)
-
-    for i in (4, 5, 6):
-        loads[i].wait()
-    arrival(held, held_recv, sibling)
-    compute(z)
-    total[...] = tokens[...].astype(jnp.float32) + part[c]
     forward(1)
+
+    @pl.when(middle)
+    def _():
+        forward(2)
 
     for i in (11, 12, 13):
         loads[i].wait()
@@ -219,30 +204,60 @@
         peer = lax.rem(ms + k, m)
         talk_copy(talk_out.at[peer], talk_in.at[ms], back_send, back_recv, peer, k).start()
 
-    def level(s, carry):
-        first = z + toward * s
-        second = z - toward * s
-
-        @pl.when(valid(first))
-        def _():
-            unit(first)
-
-        @pl.when(s + 1 < chips)
-        def _():
-            forward(s + 1)
-
-        @pl.when(valid(first))
-        def _():
-            finish(first)
-
-        @pl.when(valid(second))
-        def _():
-            unit(second)
-            finish(second)
+
+    for i in (4, 5, 6):
+        loads[i].wait()
+
+    def pair(j, carry):
+        first = order(2 * j)
+        second = order(2 * j + 1)
+
+        @pl.when(j == 1)
+        def _():
+            finish(order(1), 1)
+
+        @pl.when(j > 1)
+        def _():
+            finish(order(2 * j - 2), 0)
+            finish(order(2 * j - 1), 1)
+
+        @pl.when((j > 1) | ((j == 1) & jnp.logical_not(middle)))
+        def _():
+            forward(2 * j)
+            forward(2 * j + 1)
+
+        arrival(held, held_recv, first * CORES + 1 - c)
+        arrival(held, held_recv, second * CORES + 1 - c)
+        rows = jnp.concatenate(
+            [held[pl.ds(chip * CORES, CORES)].reshape(CORES * sessions, depth + width) for chip in (first, second)]
+        )
+        column = gate_column(rows[:, depth:].astype(jnp.float32), me, n)
+        hidden = hidden_units(rows[:, :depth], wg[...], wu[...])
+
+        @pl.when((j == 0) & middle)
+        def _():
+            forward(3)
+
+        span = min(512, depth)
+        for at in range(0, depth, span):
+            out = jnp.dot(hidden, wd[:, at : at + span], preferred_element_type=jnp.float32)
+            part[:, :, at : at + span] = (out * column).reshape(2 * CORES, sessions, span)
+        sib_out[first] = part[1 - c].astype(jnp.bfloat16)
+        sib_copy(first).start()
+        sib_out[second] = part[CORES + 1 - c].astype(jnp.bfloat16)
+        sib_copy(second).start()
+
+        @pl.when(j == 0)
+        def _():
+            total[...] = tokens[...].astype(jnp.float32) + part[c]
 
         return carry
 
-    lax.fori_loop(1, chips, level, 0)
+    pairs = chips // 2
+    lax.fori_loop(0, pairs, pair, 0)
+    if pairs > 1:
+        finish(order(chips - 2), 0)
+    finish(order(chips - 1), 1)
     arrival(sib_in, sib_recv, z)
     total[...] = total[...] + sib_in[z].astype(jnp.float32)
 
@@ -312,12 +327,16 @@
 
 
 def write_out(*refs):
-    count = len(refs) // 2
-    copies = [pltpu.make_async_copy(refs[i], refs[count + i], refs[-1].at[i]) for i in range(count)]
-    for copy in copies:
-        copy.start()
-    for copy in copies:
-        copy.wait()
+    sources, results, staged, in_sem, out_sem = refs[:4], refs[4:8], refs[8:12], refs[12], refs[13]
+    reads = [pltpu.make_async_copy(sources[i], staged[i], in_sem.at[i]) for i in range(4)]
+    writes = [pltpu.make_async_copy(staged[i], results[i], out_sem.at[i]) for i in range(4)]
+    for read in reads:
+        read.start()
+    for read, write in zip(reads, writes):
+        read.wait()
+        write.start()
+    for write in writes:
+        write.wait()
 
 
 def shards(
@@ -385,7 +404,7 @@
         + [
             dma((len(operands),)),
             pltpu.VMEM((n, sessions, depth + width), half),
-            pltpu.VMEM((CORES, sessions, depth), jnp.float32),
+            pltpu.VMEM((2 * CORES, sessions, depth), jnp.float32),
             pltpu.VMEM((chips, sessions, depth), half),
             pltpu.VMEM((chips, sessions, depth), half),
             pltpu.VMEM((chips, sessions, depth), half),
@@ -416,7 +435,7 @@
         out_shape=shapes,
         in_specs=[hbm] * len(shapes),
         out_specs=tuple(hbm for _ in shapes),
-        scratch_shapes=[dma((len(shapes),))],
+        scratch_shapes=[pltpu.VMEM(x.shape, x.dtype) for x in shapes] + [dma((4,)), dma((4,))],
         compiler_params=pltpu.CompilerParams(vmem_limit_bytes=VMEM),
     )(*results)
     return thought, spoken, audio, jnp.transpose(new_state, (1, 0, 2))

time: 51.3 us -> 33.2 us (0.65)
  Pallas kernels: 50.5 us -> 32.4 us
    pallas_call x1, Pallas kernels: 21 us -> 1.95 us  [shards(): pl.pallas_call(write_out, out_shape=shapes, in_specs=[hbm] * len(shapes),...]
    pallas_call x1, Pallas kernels: 29.5 us -> 30.5 us  [shards(): pl.pallas_call(functools.partial(kernel, n, m), out_shape=shapes, in_spec...]
where the time goes in v3:
time: 33.2 us; the launch traced here: 33.1 us
  Pallas kernels  32.4 us (98%)
  between operations  0.65 us (2%)
    pallas_call x1, Pallas kernels, shards(): pl.pallas_call(functools.partial(kernel, n, m), out_shape=shapes, in_spec...  30.5 us
    pallas_call x1, Pallas kernels, shards(): pl.pallas_call(write_out, out_shape=shapes, in_specs=[hbm] * len(shapes),...  1.95 us

profile of v3, /device:TPU:0, one launch (start us, length us, event | category | flops | bytes accessed | tf_op | source)
XLA Modules:
  0.0 33.1 jit_solution(3961265783390675080)
XLA Ops:
  0.6 30.5 %shard_map.192 = (bf16[32,2048]{1,0:T(8,128)(2,1)}, bf16[32,1024]{1,0:T(8,128)(2,1)}, bf16[32,1024]{1,0:T(8,128)(2,1)}, f32[3,32,1024]{2,1,0:T(8,128)}) custom-call(bf16[32,2048]{1,0:T(8,128)(2,1)} %refs_0_.1, f32[1,2048]{1,0:T(1,128)} %bitcast.22, s32[8,32]{1,0:T(8,128)} %bitcast.23, f32[8,32]{1,0:T(8,128)} %bitcast.24, bf16[2048,768]{1,0:T(8,128)(2,1)} %bitcast.15, ...), custom_call_target="tpu_custom_call" | custom-call | tf_op jit(solution)/shard_map/pallas_call | solution.py:396
  31.1 1.9 %shard_map.193 = (bf16[32,2048]{1,0:T(8,128)(2,1)}, bf16[32,1024]{1,0:T(8,128)(2,1)}, bf16[32,1024]{1,0:T(8,128)(2,1)}, f32[3,32,1024]{2,1,0:T(8,128)}) custom-call(bf16[32,2048]{1,0:T(8,128)(2,1)} %get-tuple-element.12.refs_0_, bf16[32,1024]{1,0:T(8,128)(2,1)} %get-tuple-element.13.refs_1_, bf16[32,1024]{1,0:T(8,128)(2,1)} %get-tuple-element.14.refs_2_, ...), custom_call_target="tpu_custom_call" | custom-call | tf_op jit(solution)/shard_map/pallas_call | solution.py:433
